TPU v7x, 32 devices: a whole 2x2x4 slice. The times are simulated.
32 devices in a mesh: row: 4 (over z), col: 8 (over y, x, core).
Axes of the slice: x: 2, y: 2, z: 4, core: 2. Of those that a mesh axis runs over, the one named last changes fastest.
Arguments:
- rhs_super: bfloat16 [2, 4, 4, 128, 512], P(None, None, 'row'), may hold values from -6 to 6
- factor_super: bfloat16 [2, 4, 4, 128, 4, 8, 128], P(None, None, 'row', None, None, 'col'), may hold values from -0.125 to 0.125
- mask_super: int32 [2, 4, 4, 4, 8], P(None, None, 'row', None, 'col'), may hold values 0 or 1
- dinv_rows: bfloat16 [4, 8, 128, 2048], P(None, 'col'), may hold values from -0.125 to 0.125
- factor_trail: bfloat16 [8, 4, 128, 4, 8, 128], P(None, 'row', None, None, 'col'), may hold values from -0.125 to 0.125
- mask_trail: int32 [8, 4, 4, 8], P(None, 'row', None, 'col'), may hold values 0 or 1
- rhs_trail: bfloat16 [8, 1, 4, 128, 512], P('col', None, 'row'), may hold values from -6 to 6
Outputs:
- solved: bfloat16 [4, 8, 128, 512], P(None, 'col')
- remaining: bfloat16 [8, 1, 4, 128, 512], P('col', None, 'row')
All inputs are finite; a program needn't handle non-finite values. No bound on the sum of `mask_super` or of `mask_trail` on one device may be relied on, other than what follows from the above.
Results may differ from a plain program's by a relative error of at most 0.0048.
Values may be sent and summed in bfloat16 or wider, within the bound.
A program may use at most 64 MiB of HBM per device.

v0:
```python
import jax
import jax.numpy as jnp
from jax import lax
from jax.sharding import PartitionSpec as P

TB = 128
ST = 16
NSB = 2


def body(rhs_super, factor_super, mask_super, dinv_rows, factor_trail, mask_trail, rhs_trail):
    width_k = rhs_super.shape[-1]
    per_col = dinv_rows.shape[0]
    per_row = rhs_super.shape[1]
    block_rows = dinv_rows.shape[-1]
    column_here = lax.axis_index("col")
    owners = (jnp.arange(per_col, dtype=jnp.int32) * lax.axis_size("col") + column_here) // ST
    solved = jnp.zeros((per_col, 1, TB, width_k), jnp.bfloat16)
    for block in range(NSB):
        due_rows = rhs_super[block]
        if block > 0:
            allowed = (owners < block).astype(jnp.int32)
            keep_tiles = (mask_super[block] * allowed[None, None, :, None]).astype(jnp.bfloat16)
            masked = factor_super[block] * keep_tiles[:, :, None, :, :, None]
            partial_sum = jnp.dot(
                masked.reshape(per_row * TB, per_col * TB),
                solved.reshape(per_col * TB, width_k),
                preferred_element_type=jnp.float32,
            )
            reached = lax.psum(partial_sum, "col")
            due_rows = (
                (due_rows.reshape(per_row * TB, width_k).astype(jnp.float32) - reached)
                .astype(jnp.bfloat16)
                .reshape(due_rows.shape)
            )
        gathered = lax.all_gather(due_rows, "row", axis=1, tiled=True).reshape(block_rows, width_k)
        columns = []
        for position in range(per_col):

            def compute(position=position):
                return jnp.dot(
                    dinv_rows[position, 0], gathered, preferred_element_type=jnp.float32
                ).astype(jnp.bfloat16)

            def retain(position=position):
                return solved[position, 0]

            columns.append(lax.cond(owners[position] == block, compute, retain))
        solved = jnp.stack(columns)[:, None]
    keep_trail = mask_trail.astype(jnp.bfloat16)[:, :, None, :, :, None]
    masked_trail = factor_trail * keep_trail
    share = rhs_trail.shape[1]
    moved = lax.all_to_all(masked_trail, "col", split_axis=0, concat_axis=4, tiled=True)
    reached = jnp.dot(
        moved.reshape(share * TB, -1),
        lax.all_gather(solved, "col", axis=1, tiled=True).reshape(-1, width_k),
        preferred_element_type=jnp.float32,
    )
    remaining = (rhs_trail.reshape(share * TB, width_k).astype(jnp.float32) - reached).astype(
        jnp.bfloat16
    )
    return (solved, remaining.reshape(rhs_trail.shape))


def solution(mesh):
    placed = (
        P(None, None, "row", None, None),
        P(None, None, "row", None, None, "col", None),
        P(None, None, "row", None, "col"),
        P(None, "col", None, None),
        P(None, "row", None, None, "col", None),
        P(None, "row", None, "col"),
        P("col", None, "row", None, None),
    )
    return jax.shard_map(
        body,
        mesh=mesh,
        in_specs=placed,
        out_specs=(P(None, "col", None, None), P("col", None, "row", None, None)),
        check_vma=False,
    )
```

profile of v0, /device:TPU:0, one launch (start us, length us, event | category | flops | bytes accessed | tf_op | source)
XLA Modules:
  0.0 228.6 jit_solution(3062503750868894067)
XLA Ops:
  7.2 0.0 slice-start
  7.2 0.0 copy-start
  7.2 0.0 all-gather.8.cloned.1.call-start
  7.2 2.2 fusion.32
  9.4 0.0 all-gather.8.cloned.1.call-update
  9.5 0.0 all-reduce.2.cloned.1.call-start
  9.5 0.7 fusion.33
  12.9 0.0 slice-done
  12.9 1.3 slice_multiply_fusion
  14.3 44.5 %all-gather.8.cloned.1.call-done = bf16[1,4,4,128,512]{4,3,2,1,0:T(8,128)(2,1)} async-done(((bf16[1,4,1,128,512]{4,3,2,1,0:T(8,128)(2,1)}), bf16[1,4,4,128,512]{4,3,2,1,0:T(8,128)(2,1)}) %all-gather.8.cloned.1.call-update) | async-done | bytes 2097168 | tf_op jit(solution)/shard_map/all_gather | solution.py:36
  58.8 0.0 copy-done
  58.9 2.1 conditional.9
  58.9 2.0 fusion.3
  61.0 2.7 %conditional.8 = (bf16[1,128,512]{2,1,0:T(8,128)(2,1)}) conditional(s32[]{:T(128)} %bitcast.21, () %tuple.72, (bf16[4,1,128,2048]{3,2,1,0:T(8,128)(2,1)S(1)}, bf16[2048,512]{1,0:T(8,128)(2,1)}) %tuple.120), branch_computations={%region_0.1_spmd, %region_1.2_spmd} | conditional | flops 268500992 | bytes 2752520 | solution.py:48
  61.0 2.7 %fusion = bf16[1,128,512]{2,1,0:T(8,128)(2,1)} fusion(bf16[2048,512]{1,0:T(8,128)(2,1)} %get-tuple-element.69, bf16[4,1,128,2048]{3,2,1,0:T(8,128)(2,1)S(1)} %get-tuple-element.68), kind=kOutput, calls=%fused_computation.1 | convolution fusion | flops 268500992 | bytes 2752512 | tf_op jit(solution)/shard_map/cond/branch_1_fun/dot_general | solution.py:41
  63.7 1.0 pad_maximum_fusion
  64.7 1.4 fusion.27
  66.1 0.0 all-reduce.2.cloned.1.call-update
  66.1 0.0 all-gather.6.cloned.1.call-start
  66.2 55.4 %all-reduce.2.cloned.1.call-done = f32[512,512]{1,0:T(8,128)} async-done(((f32[512,512]{1,0:T(8,128)}), f32[512,512]{1,0:T(8,128)}) %all-reduce.2.cloned.1.call-update) | async-done | bytes 1048592 | tf_op jit(solution)/shard_map/psum | solution.py:30
  121.6 2.2 fusion.26
  123.8 0.0 all-gather.6.cloned.1.call-update
  123.8 0.0 all-gather.10.cloned.1.call-start
  126.6 42.4 %all-gather.6.cloned.1.call-done = bf16[4,4,128,512]{3,2,0,1:T(8,128)(2,1)} async-done(((bf16[4,1,128,512]{3,2,0,1:T(8,128)(2,1)}), bf16[4,4,128,512]{3,2,0,1:T(8,128)(2,1)}) %all-gather.6.cloned.1.call-update) | async-done | bytes 2097168 | tf_op jit(solution)/shard_map/all_gather | solution.py:36
  169.0 1.8 copy.16
  170.8 1.5 conditional.15
  170.8 1.5 fusion.21
  172.3 1.5 conditional.14
  172.3 1.5 fusion.18
  173.8 0.0 copy-start.3
  173.9 0.0 copy-start.1
  173.9 1.1 pad_maximum_fusion.1
  175.0 0.0 all-gather.10.cloned.1.call-update
  175.0 0.0 copy-done.3
  175.0 0.1 copy.20
  175.1 0.4 copy-done.1
  175.5 0.7 copy.18
  176.2 0.1 broadcast_multiply_fusion
  176.3 0.0 copy-start.2
  176.4 24.5 %all_to_all.15 = bf16[8,1,128,4,1,128]{2,5,3,4,1,0:T(8,128)(2,1)S(1)} all-to-all(bf16[8,1,128,4,1,128]{2,5,3,4,1,0:T(8,128)(2,1)S(1)} %broadcast_multiply_fusion), channel_id=1, replica_groups=mesh['row'=4,'col'=8] {'col'}, dimensions={0} | all-to-all | bytes 2097152 | tf_op jit(solution)/shard_map/all_to_all | solution.py:53
  200.9 0.1 copy.19
  201.0 17.4 %all-gather.10.cloned.1.call-done = bf16[4,1024,512]{2,1,0:T(8,128)(2,1)} async-done(((bf16[4,128,512]{2,1,0:T(8,128)(2,1)}), bf16[4,1024,512]{2,1,0:T(8,128)(2,1)}) %all-gather.10.cloned.1.call-update) | async-done | bytes 4194320 | tf_op jit(solution)/shard_map/all_gather | solution.py:56
  218.4 0.0 copy-done.2
  218.4 3.6 %fusion.25 = bf16[1,1,1,128,512]{4,3,2,1,0:T(8,128)(2,1)} fusion(bf16[128,4096]{0,1:T(8,128)(2,1)S(1)} %bitcast.106, bf16[4096,512]{1,0:T(8,128)(2,1)} %bitcast.105, bf16[1,1,1,128,512]{4,3,2,1,0:T(8,128)(2,1)S(1)} %copy-done.2), kind=kOutput, calls=%fused_computation.38 | convolution fusion | flops 537067520 | bytes 5505024 | tf_op jit(solution)/shard_map/dot_general | solution.py:54
  (12 shorter events, 0.2 us)
Async XLA Ops:
  7.2 5.8 %slice-start = ((s32[2,4,1,4,1]{3,4,2,1,0:T(1,128)}), s32[1,4,1,4,1]{3,4,2,1,0:T(1,128)S(1)}, s32[]{:S(2)}) async-start(s32[2,4,1,4,1]{3,4,2,1,0:T(1,128)} %param.25), calls=%async_computation.5 | async-start | bytes 4096 | tf_op jit(solution)/shard_map/slice | solution.py:23
  7.2 51.7 %copy-start = (bf16[4,1,128,2048]{3,2,1,0:T(8,128)(2,1)S(1)}, bf16[4,1,128,2048]{3,2,1,0:T(8,128)(2,1)}, u32[]{:S(2)}) copy-start(bf16[4,1,128,2048]{3,2,1,0:T(8,128)(2,1)} %param.26) | copy-start | bytes 6291460
  7.2 51.7 %all-gather.8.cloned.1.call-start = ((), (), s32[]{:S(2)}) async-start(), calls=%async_computation.3 | async-start | bytes 2621440 | tf_op jit(solution)/shard_map/all_gather | solution.py:36
  9.5 112.2 %all-reduce.2.cloned.1.call-start = ((), (), s32[]{:S(2)}) async-start(), calls=%async_computation.1 | async-start | bytes 2097152 | tf_op jit(solution)/shard_map/psum | solution.py:30
  66.1 102.8 %all-gather.6.cloned.1.call-start = ((), (), s32[]{:S(2)}) async-start(), calls=%async_computation.2 | async-start | bytes 2621440 | tf_op jit(solution)/shard_map/all_gather | solution.py:36
  123.8 94.6 %all-gather.10.cloned.1.call-start = ((), (), s32[]{:S(2)}) async-start(), calls=%async_computation.4 | async-start | bytes 4718592 | tf_op jit(solution)/shard_map/all_gather | solution.py:56
  173.8 1.1 copy-start.3
  173.9 1.6 copy-start.1
  176.3 42.1 %copy-start.2 = (bf16[1,1,1,128,512]{4,3,2,1,0:T(8,128)(2,1)S(1)}, bf16[1,1,1,128,512]{4,3,2,1,0:T(8,128)(2,1)}, u32[]{:S(2)}) copy-start(bf16[1,1,1,128,512]{4,3,2,1,0:T(8,128)(2,1)} %param.29) | copy-start | bytes 393220
Sparse Core Ops, SparseCore 0:
  10.2 48.6 all-gather.7
  66.2 55.3 all-reduce.1
  123.9 44.9 all-gather.5
  175.1 43.2 all-gather.9
where the time goes:
time: 229 us
  waiting for transfers between devices  160 us (70%)
  blocking collectives  24.5 us (11%)
  between operations  19.4 us (8%)
  matrix products  12.7 us (6%)
  local copies, waits for them, and re-layouts  5.99 us (3%)
  other arithmetic  5.74 us (3%)
    all_gather x2, waiting for transfers between devices, body(): lax.all_gather(due_rows, 'row', axis=1, tiled=True)  86.9 us
    psum x1, waiting for transfers between devices, body(): reached = lax.psum(partial_sum, 'col')  55.4 us
    all_to_all x1, blocking collectives, body(): lax.all_to_all(masked_trail, 'col', split_axis=0, concat_axis=4, tiled=True)  24.5 us
    all_gather x1, waiting for transfers between devices, body(): lax.all_gather(solved, 'col', axis=1, tiled=True).reshape(-1, width_k)  17.4 us
    dot_general x4, matrix products, compute(): jnp.dot(dinv_rows[position, 0], gathered, preferred_element_type=jnp.floa...  7.72 us
  transfers between devices with their start and end apart: 4, of which 4 were waited for; matrix products, arithmetic and copies ran while one was open for 1% of the time, Pallas kernels for 0%

commit v1 on v0

--- a/solution.py
+++ b/solution.py
@@ -1,6 +1,10 @@
+import functools
+
 import jax
 import jax.numpy as jnp
 from jax import lax
+from jax.experimental import pallas as pl
+from jax.experimental.pallas import tpu as pltpu
 from jax.sharding import PartitionSpec as P
 
 TB = 128
@@ -8,7 +12,7 @@
 NSB = 2
 
 
-def body(rhs_super, factor_super, mask_super, dinv_rows, factor_trail, mask_trail, rhs_trail):
+def plain_body(rhs_super, factor_super, mask_super, dinv_rows, factor_trail, mask_trail, rhs_trail):
     width_k = rhs_super.shape[-1]
     per_col = dinv_rows.shape[0]
     per_row = rhs_super.shape[1]
@@ -62,6 +66,264 @@
     return (solved, remaining.reshape(rhs_trail.shape))
 
 
+MESH = pl.DeviceIdType.MESH
+F32 = jnp.float32
+BF16 = jnp.bfloat16
+
+
+def kernel(
+    n_row, n_col,
+    rhs_s, fac_s, mask_s, dinv, fac_t, mask_t, rhs_t,
+    solved_o, rem_o,
+    dinv_v, facs_v, fact_v, rhst_v, ltri, due0, due1, share1, part, rs0, solv, lt, acc, tpart, trs,
+    local_sem, z_send, z_recv, l_send, l_recv, g_send, g_recv, p_send, p_recv, s_send, s_recv, t_send, t_recv,
+):
+    per_sb = dinv_v.shape[0] // NSB
+    per_col = dinv_v.shape[0]
+    sq_count, halves, sh, kr = due0.shape[0], due0.shape[2], due0.shape[3], due0.shape[4]
+    tiles_t = lt.shape[0] // TB
+    cols = per_sb * TB
+    r, c = lax.axis_index("row"), lax.axis_index("col")
+    sq, half = c // halves, c % halves
+    rows_at = lambda d: lax.rem(r + d, n_row)
+    cols_at = lambda d: lax.rem(c + d, n_col)
+
+    barrier = pltpu.get_barrier_semaphore()
+    for d in range(1, n_row):
+        pl.semaphore_signal(barrier, inc=1, device_id=(rows_at(d), c), device_id_type=MESH)
+    for d in range(1, n_col):
+        pl.semaphore_signal(barrier, inc=1, device_id=(r, cols_at(d)), device_id_type=MESH)
+
+    def kslice(k):
+        return pl.ds(pl.multiple_of(k * kr, kr), kr)
+
+    own_rows = pl.ds(pl.multiple_of(half * sh, sh), sh)
+    local = [
+        pltpu.make_async_copy(fac_s.at[1], facs_v, local_sem.at[0]),
+        pltpu.make_async_copy(rhs_s.at[0, sq, own_rows, kslice(r)], due0.at[sq, r, half], local_sem.at[1]),
+        pltpu.make_async_copy(rhs_s.at[1, sq, own_rows, kslice(r)], share1.at[r], local_sem.at[2]),
+        pltpu.make_async_copy(dinv, dinv_v, local_sem.at[3]),
+        pltpu.make_async_copy(fac_t, fact_v, local_sem.at[4]),
+        pltpu.make_async_copy(rhs_t, rhst_v, local_sem.at[5]),
+    ]
+    for copy in local:
+        copy.start()
+    pl.semaphore_wait(barrier, n_row - 1 + n_col - 1)
+
+    def remote(src, dst, send, recv, device):
+        copy = pltpu.make_async_remote_copy(
+            src_ref=src, dst_ref=dst, send_sem=send, recv_sem=recv, device_id=device, device_id_type=MESH
+        )
+        copy.start()
+        return copy
+
+    z_copies = []
+    for s in range(NSB):
+        for d in range(1, n_row):
+            to = rows_at(d)
+            dst = due0.at[sq, r, half] if s == 0 else share1.at[r]
+            z_copies.append(remote(
+                rhs_s.at[s, sq, own_rows, kslice(to)], dst, z_send.at[s, d - 1], z_recv.at[s, d - 1], (to, c)))
+
+    def sorter(count):
+        shape = (count * TB, per_col * TB)
+        a = lax.broadcasted_iota(jnp.int32, shape, 0)
+        b = lax.broadcasted_iota(jnp.int32, shape, 1)
+        return (b == (a % TB) * per_col + a // TB).astype(F32).astype(BF16)
+
+    local[0].wait()
+    sort_few = sorter(per_sb)
+    for q in range(sq_count):
+        tiles = jnp.dot(sort_few, facs_v[q], preferred_element_type=F32)
+        for p in range(per_sb):
+            kept = tiles[p * TB:(p + 1) * TB] * mask_s[1, q, p].astype(F32)
+            ltri[r, q, :, p * TB:(p + 1) * TB] = kept.astype(BF16)
+    l_copies = [
+        remote(ltri.at[r], ltri.at[r], l_send.at[d - 1], l_recv.at[d - 1], (rows_at(d), c)) for d in range(1, n_row)
+    ]
+
+    def gather(due, s):
+        return [
+            remote(due.at[sq, :, half], due.at[sq, :, half], g_send.at[s, d - 1], g_recv.at[s, d - 1], (r, cols_at(d)))
+            for d in range(1, n_col)
+        ]
+
+    def spread(s):
+        return [
+            remote(solv.at[s, r], solv.at[s, r], s_send.at[s, d - 1], s_recv.at[s, d - 1], (rows_at(d), c))
+            for d in range(1, n_row)
+        ]
+
+    def solve(due, s):
+        block = dinv_v[s * per_sb:(s + 1) * per_sb].reshape(cols, -1)
+        fresh = jnp.dot(block, due[...].reshape(-1, kr), preferred_element_type=F32).astype(BF16)
+        solv[s, r] = fresh
+        return fresh
+
+    local[1].wait()
+    for copy in z_copies[:n_row - 1]:
+        copy.wait_recv()
+    g0 = gather(due0, 0)
+    local[3].wait()
+    for copy in g0:
+        copy.wait_recv()
+    fresh = solve(due0, 0)
+    s0 = spread(0)
+
+    for d in range(n_row):
+        at = rows_at(n_row - d)
+        if d > 0:
+            l_copies[d - 1].wait_recv()
+        update = jnp.dot(ltri[at].reshape(-1, cols), fresh, preferred_element_type=F32).astype(BF16)
+        part[:, at] = update.reshape(sq_count, halves, sh, kr)
+    p_copies = []
+    for d in range(1, n_col):
+        to = cols_at(d)
+        p_copies.append(remote(
+            part.at[to // halves, :, to % halves], rs0.at[d - 1], p_send.at[d - 1], p_recv.at[d - 1], (r, to)))
+
+    local[4].wait()
+    sort_all = sorter(per_col)
+
+    def order(i, _):
+        tiles = jnp.dot(sort_all, fact_v[i], preferred_element_type=F32)
+        for p in range(per_col):
+            kept = tiles[p * TB:(p + 1) * TB] * mask_t[i, p].astype(F32)
+            lt[pl.ds(pl.multiple_of(i * TB, TB), TB), p * TB:(p + 1) * TB] = kept.astype(BF16)
+        return 0
+
+    lax.fori_loop(0, tiles_t, order, 0)
+
+    local[2].wait()
+    for copy in z_copies[n_row - 1:]:
+        copy.wait_recv()
+    reached = part[sq, :, half].astype(F32)
+    for d in range(1, n_col):
+        p_copies[d - 1].wait_recv()
+        reached += rs0[d - 1].astype(F32)
+    due1[sq, :, half] = (share1[...].astype(F32) - reached).astype(BF16)
+    g1 = gather(due1, 1)
+
+    for d in range(n_row):
+        at = rows_at(n_row - d)
+        if d > 0:
+            s0[d - 1].wait_recv()
+        acc[at] = jnp.dot(lt[:, :cols], solv[0, at], preferred_element_type=F32)
+
+    for copy in g1:
+        copy.wait_recv()
+    solve(due1, 1)
+    s1 = spread(1)
+
+    t_copies = []
+    for d in range(n_row):
+        at = rows_at(n_row - d)
+        if d > 0:
+            s1[d - 1].wait_recv()
+        update = acc[at] + jnp.dot(lt[:, cols:], solv[1, at], preferred_element_type=F32)
+        tpart[at] = update.astype(BF16).reshape(n_col, -1, kr)
+        t_copies.append([
+            remote(tpart.at[at, cols_at(e)], trs.at[d, e - 1], t_send.at[d, e - 1], t_recv.at[d, e - 1], (r, cols_at(e)))
+            for e in range(1, n_col)
+        ])
+    for s in range(NSB):
+        for k in range(n_row):
+            solved_o[s * per_sb:(s + 1) * per_sb, :, k * kr:(k + 1) * kr] = solv[s, k].reshape(per_sb, TB, kr)
+    local[5].wait()
+    for d in range(n_row):
+        at = rows_at(n_row - d)
+        reached = tpart[at, c].astype(F32)
+        for e in range(1, n_col):
+            t_copies[d][e - 1].wait_recv()
+            reached += trs[d, e - 1].astype(F32)
+        rem_o[:, kslice(at)] = (rhst_v[:, kslice(at)].astype(F32) - reached).astype(BF16)
+
+    for copy in z_copies + l_copies + g0 + s0 + p_copies + g1 + s1 + sum(t_copies, []):
+        copy.wait_send()
+
+
+def fast_body(n_row, n_col, rhs_super, factor_super, mask_super, dinv_rows, factor_trail, mask_trail, rhs_trail):
+    width_k = rhs_super.shape[-1]
+    sq_count = rhs_super.shape[1]
+    per_col = dinv_rows.shape[0]
+    tiles_t = factor_trail.shape[0]
+    share_t = rhs_trail.shape[1]
+    per_sb = per_col // NSB
+    cols = per_sb * TB
+    kr = width_k // n_row
+    sh = sq_count * TB // n_col
+    halves = TB // sh
+    vmem = lambda *shape: pltpu.VMEM(shape, BF16)
+    dma = lambda *shape: pltpu.SemaphoreType.DMA(shape)
+    due_shape = (sq_count, n_row, halves, sh, kr)
+    anywhere = pl.BlockSpec(memory_space=pl.ANY)
+    scalars = pl.BlockSpec(memory_space=pltpu.SMEM)
+    whole = pl.BlockSpec(memory_space=pltpu.VMEM)
+    solved, remaining = pl.pallas_call(
+        functools.partial(kernel, n_row, n_col),
+        out_shape=(
+            jax.ShapeDtypeStruct((per_col, TB, width_k), BF16),
+            jax.ShapeDtypeStruct((share_t * TB, width_k), BF16),
+        ),
+        in_specs=[anywhere, anywhere, scalars, anywhere, anywhere, scalars, anywhere],
+        out_specs=(whole, whole),
+        scratch_shapes=[
+            vmem(per_col, TB, dinv_rows.shape[-1]),
+            vmem(sq_count, TB * per_col, TB),
+            vmem(tiles_t, TB * per_col, TB),
+            vmem(share_t * TB, width_k),
+            vmem(n_row, sq_count, TB, cols),
+            vmem(*due_shape),
+            vmem(*due_shape),
+            vmem(n_row, sh, kr),
+            vmem(*due_shape),
+            vmem(n_col - 1, n_row, sh, kr),
+            vmem(NSB, n_row, cols, kr),
+            vmem(tiles_t * TB, per_col * TB),
+            pltpu.VMEM((n_row, tiles_t * TB, kr), F32),
+            vmem(n_row, n_col, share_t * TB, kr),
+            vmem(n_row, n_col - 1, share_t * TB, kr),
+            dma(6),
+            dma(NSB, n_row - 1), dma(NSB, n_row - 1),
+            dma(n_row - 1), dma(n_row - 1),
+            dma(NSB, n_col - 1), dma(NSB, n_col - 1),
+            dma(n_col - 1), dma(n_col - 1),
+            dma(NSB, n_row - 1), dma(NSB, n_row - 1),
+            dma(n_row, n_col - 1), dma(n_row, n_col - 1),
+        ],
+        compiler_params=pltpu.CompilerParams(
+            collective_id=0, has_side_effects=True, vmem_limit_bytes=40 * 1024 * 1024
+        ),
+    )(
+        rhs_super.reshape(NSB, sq_count, TB, width_k),
+        factor_super.reshape(NSB, sq_count, TB * per_col, TB),
+        mask_super.reshape(NSB, sq_count, per_col),
+        dinv_rows.reshape(per_col, TB, -1),
+        factor_trail.reshape(tiles_t, TB * per_col, TB),
+        mask_trail.reshape(tiles_t, per_col),
+        rhs_trail.reshape(share_t * TB, width_k),
+    )
+    return solved[:, None], remaining.reshape(rhs_trail.shape)
+
+
+def body_for(mesh):
+    n_row, n_col = mesh.shape["row"], mesh.shape["col"]
+
+    def body(rhs_super, factor_super, mask_super, dinv_rows, factor_trail, mask_trail, rhs_trail):
+        args = (rhs_super, factor_super, mask_super, dinv_rows, factor_trail, mask_trail, rhs_trail)
+        due_rows = rhs_super.shape[1] * TB
+        fits = (
+            ST % n_col == 0
+            and due_rows % n_col == 0
+            and TB % (due_rows // n_col) == 0
+            and (due_rows // n_col) % 16 == 0
+            and rhs_super.shape[-1] % (n_row * 128) == 0
+        )
+        return fast_body(n_row, n_col, *args) if fits else plain_body(*args)
+
+    return body
+
+
 def solution(mesh):
     placed = (
         P(None, None, "row", None, None),
@@ -73,7 +335,7 @@
         P("col", None, "row", None, None),
     )
     return jax.shard_map(
-        body,
+        body_for(mesh),
         mesh=mesh,
         in_specs=placed,
         out_specs=(P(None, "col", None, None), P("col", None, "row", None, None)),

time: 229 us -> 77 us (0.34)
  waiting for transfers between devices: 160 us -> 0 us
  Pallas kernels: 0 us -> 67 us
  blocking collectives: 24.5 us -> 0 us
  between operations: 19.4 us -> 0.64 us
  matrix products: 12.7 us -> 0 us
  other arithmetic: 5.74 us -> 0 us
  local copies, waits for them, and re-layouts: 5.99 us -> 9.06 us
    all_gather x3 -> x0, waiting for transfers between devices: 104 us -> none  [the longest x2 86.9 us: body(): lax.all_gather(due_rows, 'row', axis=1, tiled=True)]
    pallas_call x0 -> x1, Pallas kernels: none -> 67 us  [fast_body(): pl.pallas_call(functools.partial(kernel, n_row, n_col), out_shape=(jax.Sh...]
    psum x1 -> x0, waiting for transfers between devices: 55.4 us -> none  [body(): reached = lax.psum(partial_sum, 'col')]
    all_to_all x1 -> x0, blocking collectives: 24.5 us -> none  [body(): lax.all_to_all(masked_trail, 'col', split_axis=0, concat_axis=4, tiled=True)]
    dot_general x6 -> x0, matrix products: 12.7 us -> none  [the longest x4 7.72 us: compute(): jnp.dot(dinv_rows[position, 0], gathered, preferred_element_type=jnp.floa...]
    unnamed x9 -> x14, local copies, waits for them, and re-layouts: 1.09 us -> 8.3 us
    slice x4 -> x0, local copies, waits for them, and re-layouts: 2.87 us -> none  [the longest x1 2.2 us: body(): due_rows = rhs_super[block]]
  transfers between devices with their start and end apart: 4 -> 0, of which waited for: 4 -> 0; matrix products, arithmetic and copies ran while one was open for 1% -> 0% of each run, Pallas kernels for 0% -> 0%
where the time goes in v1:
time: 77 us; the launch traced here: 76.7 us
  Pallas kernels  67 us (87%)
  local copies, waits for them, and re-layouts  9.06 us (12%)
    pallas_call x1, Pallas kernels, fast_body(): pl.pallas_call(functools.partial(kernel, n_row, n_col), out_shape=(jax.Sh...  67 us
    unnamed x14, local copies, waits for them, and re-layouts  8.3 us

profile of v1, /device:TPU:0, one launch (start us, length us, event | category | flops | bytes accessed | tf_op | source)
XLA Modules:
  0.0 76.7 jit_solution(10901104075575816959)
XLA Ops:
  0.6 0.8 copy.9.mask_t
  1.4 0.0 copy-start
  1.4 1.6 %copy-done = bf16[4,1,128,2048]{3,2,1,0:T(8,128)(2,1)S(1)} copy-done((bf16[4,1,128,2048]{3,2,1,0:T(8,128)(2,1)S(1)}, bf16[4,1,128,2048]{3,2,1,0:T(8,128)(2,1)}, u32[]{:S(2)}) %copy-start) | copy-done | bytes 2097176
  3.0 0.0 copy-start.1
  3.0 1.2 %copy-done.1 = bf16[2,4,1,128,512]{4,3,2,1,0:T(8,128)(2,1)S(1)} copy-done((bf16[2,4,1,128,512]{4,3,2,1,0:T(8,128)(2,1)S(1)}, bf16[2,4,1,128,512]{4,3,2,1,0:T(8,128)(2,1)}, u32[]{:S(2)}) %copy-start.1) | copy-done | bytes 1048600
  4.2 0.0 copy-start.2
  4.2 1.2 %copy-done.2 = bf16[2,4,1,128,4,1,128]{6,4,5,3,2,1,0:T(4,128)(2,1)S(1)} copy-done((bf16[2,4,1,128,4,1,128]{6,4,5,3,2,1,0:T(4,128)(2,1)S(1)}, bf16[2,4,1,128,4,1,128]{6,4,5,3,2,1,0:T(4,128)(2,1)}, u32[]{:S(2)}) %copy-start.2) | copy-done | bytes 1048600
  5.4 0.0 copy-start.3
  5.4 1.2 %copy-done.3 = bf16[8,1,128,4,1,128]{5,3,4,2,1,0:T(4,128)(2,1)S(1)} copy-done((bf16[8,1,128,4,1,128]{5,3,4,2,1,0:T(4,128)(2,1)S(1)}, bf16[8,1,128,4,1,128]{5,3,4,2,1,0:T(4,128)(2,1)}, u32[]{:S(2)}) %copy-start.3) | copy-done | bytes 1048600
  6.7 0.0 copy-start.4
  6.7 0.9 %copy-done.4 = bf16[1,1,1,128,512]{4,3,2,1,0:T(8,128)(2,1)S(1)} copy-done((bf16[1,1,1,128,512]{4,3,2,1,0:T(8,128)(2,1)S(1)}, bf16[1,1,1,128,512]{4,3,2,1,0:T(8,128)(2,1)}, u32[]{:S(2)}) %copy-start.4) | copy-done | bytes 131096
  7.6 0.0 copy-start.5
  7.6 0.7 copy-done.5
  8.2 67.0 %shard_map.86 = (bf16[4,128,512]{2,1,0:T(8,128)(2,1)S(1)}, bf16[128,512]{1,0:T(8,128)(2,1)S(1)}) custom-call(bf16[2,4,128,512]{3,2,1,0:T(8,128)(2,1)S(1)} %bitcast.12, bf16[2,4,512,128]{3,2,1,0:T(8,128)(2,1)S(1)} %bitcast.13, s32[2,4,4]{2,1,0:T(4,128)S(1)} %bitcast.18, bf16[4,128,2048]{2,1,0:T(8,128)(2,1)S(1)} %bitcast.11, ...), custom_call_target="tpu_custom_call" | custom-call | tf_op jit(solution)/shard_map/pallas_call | solution.py:262
  75.2 0.8 %copy.13 = bf16[4,1,128,512]{3,2,1,0:T(8,128)(2,1)} copy(bf16[4,1,128,512]{3,2,1,0:T(8,128)(2,1)S(1)} %bitcast.15) | data formatting | bytes 1048576
  76.0 0.7 copy.14
Async XLA Ops:
  1.4 1.6 %copy-start = (bf16[4,1,128,2048]{3,2,1,0:T(8,128)(2,1)S(1)}, bf16[4,1,128,2048]{3,2,1,0:T(8,128)(2,1)}, u32[]{:S(2)}) copy-start(bf16[4,1,128,2048]{3,2,1,0:T(8,128)(2,1)} %param.10) | copy-start | bytes 6291460
  3.0 1.2 %copy-start.1 = (bf16[2,4,1,128,512]{4,3,2,1,0:T(8,128)(2,1)S(1)}, bf16[2,4,1,128,512]{4,3,2,1,0:T(8,128)(2,1)}, u32[]{:S(2)}) copy-start(bf16[2,4,1,128,512]{4,3,2,1,0:T(8,128)(2,1)} %param.7) | copy-start | bytes 3145732
  4.2 1.2 %copy-start.2 = (bf16[2,4,1,128,4,1,128]{6,4,5,3,2,1,0:T(4,128)(2,1)S(1)}, bf16[2,4,1,128,4,1,128]{6,4,5,3,2,1,0:T(4,128)(2,1)}, u32[]{:S(2)}) copy-start(bf16[2,4,1,128,4,1,128]{6,4,5,3,2,1,0:T(4,128)(2,1)} %param.8) | copy-start | bytes 3145732
  5.4 1.2 %copy-start.3 = (bf16[8,1,128,4,1,128]{5,3,4,2,1,0:T(4,128)(2,1)S(1)}, bf16[8,1,128,4,1,128]{5,3,4,2,1,0:T(4,128)(2,1)}, u32[]{:S(2)}) copy-start(bf16[8,1,128,4,1,128]{5,3,4,2,1,0:T(4,128)(2,1)} %param.11) | copy-start | bytes 3145732
  6.7 0.9 %copy-start.4 = (bf16[1,1,1,128,512]{4,3,2,1,0:T(8,128)(2,1)S(1)}, bf16[1,1,1,128,512]{4,3,2,1,0:T(8,128)(2,1)}, u32[]{:S(2)}) copy-start(bf16[1,1,1,128,512]{4,3,2,1,0:T(8,128)(2,1)} %param.13) | copy-start | bytes 393220
  7.6 0.7 copy-start.5

commit v2 on v1

v2 whole, which is shorter than its diff:
```python
import functools

import jax
import jax.numpy as jnp
from jax import lax
from jax.experimental import pallas as pl
from jax.experimental.pallas import tpu as pltpu
from jax.sharding import PartitionSpec as P

TB = 128
ST = 16
NSB = 2


def plain_body(rhs_super, factor_super, mask_super, dinv_rows, factor_trail, mask_trail, rhs_trail):
    width_k = rhs_super.shape[-1]
    per_col = dinv_rows.shape[0]
    per_row = rhs_super.shape[1]
    block_rows = dinv_rows.shape[-1]
    column_here = lax.axis_index("col")
    owners = (jnp.arange(per_col, dtype=jnp.int32) * lax.axis_size("col") + column_here) // ST
    solved = jnp.zeros((per_col, 1, TB, width_k), jnp.bfloat16)
    for block in range(NSB):
        due_rows = rhs_super[block]
        if block > 0:
            allowed = (owners < block).astype(jnp.int32)
            keep_tiles = (mask_super[block] * allowed[None, None, :, None]).astype(jnp.bfloat16)
            masked = factor_super[block] * keep_tiles[:, :, None, :, :, None]
            partial_sum = jnp.dot(
                masked.reshape(per_row * TB, per_col * TB),
                solved.reshape(per_col * TB, width_k),
                preferred_element_type=jnp.float32,
            )
            reached = lax.psum(partial_sum, "col")
            due_rows = (
                (due_rows.reshape(per_row * TB, width_k).astype(jnp.float32) - reached)
                .astype(jnp.bfloat16)
                .reshape(due_rows.shape)
            )
        gathered = lax.all_gather(due_rows, "row", axis=1, tiled=True).reshape(block_rows, width_k)
        columns = []
        for position in range(per_col):

            def compute(position=position):
                return jnp.dot(
                    dinv_rows[position, 0], gathered, preferred_element_type=jnp.float32
                ).astype(jnp.bfloat16)

            def retain(position=position):
                return solved[position, 0]

            columns.append(lax.cond(owners[position] == block, compute, retain))
        solved = jnp.stack(columns)[:, None]
    keep_trail = mask_trail.astype(jnp.bfloat16)[:, :, None, :, :, None]
    masked_trail = factor_trail * keep_trail
    share = rhs_trail.shape[1]
    moved = lax.all_to_all(masked_trail, "col", split_axis=0, concat_axis=4, tiled=True)
    reached = jnp.dot(
        moved.reshape(share * TB, -1),
        lax.all_gather(solved, "col", axis=1, tiled=True).reshape(-1, width_k),
        preferred_element_type=jnp.float32,
    )
    remaining = (rhs_trail.reshape(share * TB, width_k).astype(jnp.float32) - reached).astype(
        jnp.bfloat16
    )
    return (solved, remaining.reshape(rhs_trail.shape))


MESH = pl.DeviceIdType.MESH
F32 = jnp.float32
BF16 = jnp.bfloat16


def kernel(
    n_row, n_col,
    rhs_s, fac_s, mask_s, dinv, fac_t, mask_t, rhs_t,
    solved_o, rem_o,
    dinv_v, facs_v, fact_v, rhst_v, rhs1_v, ltri, due0, due1, dsh, part, rs0, solv, lt, acc, tpart, trs,
    local_sem, pair_send, pair_recv, z_send, z_recv, g_send, g_recv, f_send, f_recv, p_send, p_recv,
    s_send, s_recv, e_send, e_recv, t_send, t_recv,
):
    per_sb = dinv_v.shape[0] // NSB
    per_col = dinv_v.shape[0]
    sq_count, halves, sh, kr = due0.shape[0], due0.shape[2], due0.shape[3], due0.shape[4]
    sh2 = sh // 2
    tiles_t = fact_v.shape[0]
    share_t = tiles_t // n_col
    th = TB // 2
    cols = per_sb * TB
    n_chip = n_col // 2
    r, c = lax.axis_index("row"), lax.axis_index("col")
    chip, core = c // 2, c % 2
    other = 1 - core
    sib = chip * 2 + other
    sq, half = c // halves, c % halves
    rows_at = lambda d: lax.rem(r + d, n_row)
    cols_at = lambda d: lax.rem(c + d, n_col)

    barrier = pltpu.get_barrier_semaphore()
    for d in range(1, n_row):
        pl.semaphore_signal(barrier, inc=1, device_id=(rows_at(d), c), device_id_type=MESH)
    for d in range(1, n_col):
        pl.semaphore_signal(barrier, inc=1, device_id=(r, cols_at(d)), device_id_type=MESH)

    def kslice(k):
        return pl.ds(pl.multiple_of(k * kr, kr), kr)

    own_rows = pl.ds(pl.multiple_of(half * sh, sh), sh)
    local = [
        pltpu.make_async_copy(fac_s.at[1], facs_v, local_sem.at[0]),
        pltpu.make_async_copy(rhs_s.at[0, sq, own_rows, kslice(r)], due0.at[sq, r, half], local_sem.at[1]),
        pltpu.make_async_copy(fac_t, fact_v, local_sem.at[2]),
        pltpu.make_async_copy(dinv, dinv_v, local_sem.at[3]),
    ]
    for k in range(2):
        rows = pl.ds(pl.multiple_of(half * sh + k * sh2, sh2), sh2)
        local.append(pltpu.make_async_copy(rhs_s.at[1, sq, rows], rhs1_v.at[k], local_sem.at[4 + k]))
    local.append(pltpu.make_async_copy(rhs_t, rhst_v, local_sem.at[6]))
    for copy in local:
        copy.start()

    def sorter(count):
        shape = (count * TB, per_col * TB)
        a = lax.broadcasted_iota(jnp.int32, shape, 0)
        b = lax.broadcasted_iota(jnp.int32, shape, 1)
        return (b == (a % TB) * per_col + a // TB).astype(F32).astype(BF16)

    sort_all = sorter(per_col)
    local[0].wait()
    for q in range(sq_count):
        tiles = jnp.dot(sort_all[:cols], facs_v[q], preferred_element_type=F32)
        for p in range(per_sb):
            kept = (tiles[p * TB:(p + 1) * TB] * mask_s[1, q, p].astype(F32)).astype(BF16)
            for h in range(halves):
                for k in range(2):
                    at = (q * halves + h) * sh2
                    ltri[k, core, at:at + sh2, p * TB:(p + 1) * TB] = kept[h * sh + k * sh2:h * sh + (k + 1) * sh2]
    pl.semaphore_wait(barrier, n_row - 1 + n_col - 1)
    started = []

    def remote(src, dst, send, recv, device):
        copy = pltpu.make_async_remote_copy(
            src_ref=src, dst_ref=dst, send_sem=send, recv_sem=recv, device_id=device, device_id_type=MESH
        )
        started.append(copy)
        copy.start()
        return copy

    z0 = [
        remote(rhs_s.at[0, sq, own_rows, kslice(rows_at(d))], due0.at[sq, r, half],
               z_send.at[0, d - 1], z_recv.at[0, d - 1], (rows_at(d), c))
        for d in range(1, n_row)
    ]
    pair_l = remote(ltri.at[other, core], ltri.at[other, core], pair_send.at[0], pair_recv.at[0], (r, sib))

    def gather(due, s):
        own = due.at[sq, :, half]
        copies = [
            remote(own, own, g_send.at[s, e], g_recv.at[s, e], (r, lax.rem(chip + e, n_chip) * 2 + core))
            for e in range(1, n_chip)
        ]
        return [remote(own, own, g_send.at[s, 0], g_recv.at[s, 0], (r, sib))] + copies

    def gathered(due, s, copies):
        passed = []
        for e in range(1, n_chip):
            copies[e].wait_recv()
            came = lax.rem(chip + n_chip - e, n_chip) * 2 + core
            slot = due.at[came // halves, :, came % halves]
            passed.append(remote(slot, slot, f_send.at[s, e - 1], f_recv.at[s, e - 1], (r, sib)))
        copies[0].wait_recv()
        for copy in passed:
            copy.wait_recv()

    def solve(due, s):
        block = dinv_v[s * per_sb:(s + 1) * per_sb].reshape(cols, -1)
        fresh = jnp.dot(block, due[...].reshape(-1, kr), preferred_element_type=F32)
        solv[s, r, core] = fresh.astype(BF16)
        own = solv.at[s, r, core]
        near = remote(own, own, e_send.at[s, 0], e_recv.at[s, 0], (r, sib))
        return [near] + [
            remote(own, own, s_send.at[s, d - 1], s_recv.at[s, d - 1], (rows_at(d), c)) for d in range(1, n_row)
        ]

    def slice_ready(s, d, copies):
        copies[d].wait_recv()
        if d > 0:
            slot = solv.at[s, rows_at(n_row - d), core]
            remote(slot, slot, e_send.at[s, d], e_recv.at[s, d], (r, sib)).wait_recv()

    local[1].wait()
    for copy in z0:
        copy.wait_recv()
    g0 = gather(due0, 0)

    local[2].wait()

    def order(i, _):
        tiles = jnp.dot(sort_all, fact_v[i], preferred_element_type=F32)
        for p in range(per_col):
            kept = (tiles[p * TB:(p + 1) * TB] * mask_t[p, i].astype(F32)).astype(BF16)
            for k in range(2):
                lt[k, core, pl.ds(pl.multiple_of(i * th, th), th), p * TB:(p + 1) * TB] = kept[k * th:(k + 1) * th]
        return 0

    lax.fori_loop(0, tiles_t, order, 0)
    local[3].wait()
    gathered(due0, 0, g0)
    s0 = solve(due0, 0)
    pair_l.wait_recv()
    local[4].wait()
    local[5].wait()

    p_copies = []
    for d in range(n_row):
        at = rows_at(n_row - d)
        slice_ready(0, d, s0)
        update = jnp.dot(ltri[core, 0], solv[0, at, 0], preferred_element_type=F32)
        update += jnp.dot(ltri[core, 1], solv[0, at, 1], preferred_element_type=F32)
        part[at] = update.astype(BF16).reshape(n_col, sh2, kr)
        p_copies.append([
            remote(part.at[at, cols_at(e)], rs0.at[d, e - 1], p_send.at[d, e - 1], p_recv.at[d, e - 1], (r, cols_at(e)))
            for e in range(1, n_col)
        ])
    pair_t = remote(lt.at[other, core], lt.at[other, core], pair_send.at[1], pair_recv.at[1], (r, sib))

    def total(own, landed, copies):
        same, far = own.astype(F32), None
        for e in range(1, n_col):
            copies[e - 1].wait_recv()
            came = landed[e - 1].astype(F32)
            if e % 2 == 0:
                same += came
            else:
                far = came if far is None else far + came
        return same, far

    z1 = []
    for d in range(n_row):
        at = rows_at(n_row - d)
        for k, reached in zip((core, other), total(part[at, c], rs0.at[d], p_copies[d])):
            due = (rhs1_v[k, :, kslice(at)].astype(F32) - reached).astype(BF16)
            if d == 0:
                due1[sq, r, half, k] = due
            else:
                dsh[at, k] = due
        if d > 0:
            z1.append(remote(dsh.at[at], due1.at[sq, r, half], z_send.at[1, d - 1], z_recv.at[1, d - 1], (at, c)))
    for copy in z1:
        copy.wait_recv()
    g1 = gather(due1, 1)

    pair_t.wait_recv()
    for k in range(n_row):
        update = jnp.dot(lt[core, 0, :, :cols], solv[0, k, 0], preferred_element_type=F32)
        acc[k] = update + jnp.dot(lt[core, 1, :, :cols], solv[0, k, 1], preferred_element_type=F32)
    gathered(due1, 1, g1)
    s1 = solve(due1, 1)

    t_copies = []
    for d in range(n_row):
        at = rows_at(n_row - d)
        slice_ready(1, d, s1)
        update = acc[at] + jnp.dot(lt[core, 0, :, cols:], solv[1, at, 0], preferred_element_type=F32)
        update += jnp.dot(lt[core, 1, :, cols:], solv[1, at, 1], preferred_element_type=F32)
        tpart[at] = update.astype(BF16).reshape(n_col, -1, kr)
        t_copies.append([
            remote(tpart.at[at, cols_at(e)], trs.at[d, e - 1], t_send.at[d, e - 1], t_recv.at[d, e - 1], (r, cols_at(e)))
            for e in range(1, n_col)
        ])
    for s in range(NSB):
        for k in range(n_row):
            for_core = solv[s, k, core]
            solved_o[s * per_sb:(s + 1) * per_sb, :, k * kr:(k + 1) * kr] = for_core.reshape(per_sb, TB, kr)
    local[6].wait()
    for d in range(n_row):
        at = rows_at(n_row - d)
        for k, reached in zip((core, other), total(tpart[at, c], trs.at[d], t_copies[d])):
            for t in range(share_t):
                here = rhst_v[t, k, :, kslice(at)].astype(F32) - reached[t * th:(t + 1) * th]
                rem_o[t, k, :, kslice(at)] = here.astype(BF16)
    for copy in started:
        copy.wait_send()


def fast_body(n_row, n_col, rhs_super, factor_super, mask_super, dinv_rows, factor_trail, mask_trail, rhs_trail):
    width_k = rhs_super.shape[-1]
    sq_count = rhs_super.shape[1]
    per_col = dinv_rows.shape[0]
    tiles_t = factor_trail.shape[0]
    share_t = rhs_trail.shape[1]
    per_sb = per_col // NSB
    cols = per_sb * TB
    kr = width_k // n_row
    sh = sq_count * TB // n_col
    halves = TB // sh
    vmem = lambda *shape: pltpu.VMEM(shape, BF16)
    dma = lambda *shape: pltpu.SemaphoreType.DMA(shape)
    sh2, th, n_chip = sh // 2, TB // 2, n_col // 2
    anywhere = pl.BlockSpec(memory_space=pl.ANY)
    scalars = pl.BlockSpec(memory_space=pltpu.SMEM)
    whole = pl.BlockSpec(memory_space=pltpu.VMEM)
    solved, remaining = pl.pallas_call(
        functools.partial(kernel, n_row, n_col),
        out_shape=(
            jax.ShapeDtypeStruct((per_col, TB, width_k), BF16),
            jax.ShapeDtypeStruct((share_t, 2, th, width_k), BF16),
        ),
        in_specs=[anywhere, anywhere, scalars, anywhere, anywhere, scalars, anywhere],
        out_specs=(whole, whole),
        scratch_shapes=[
            vmem(per_col, TB, dinv_rows.shape[-1]),
            vmem(sq_count, TB * per_col, TB),
            vmem(tiles_t, TB * per_col, TB),
            vmem(share_t, 2, th, width_k),
            vmem(2, sh2, width_k),
            vmem(2, 2, n_col * sh2, cols),
            vmem(sq_count, n_row, halves, sh, kr),
            vmem(sq_count, n_row, halves, 2, sh2, kr),
            vmem(n_row, 2, sh2, kr),
            vmem(n_row, n_col, sh2, kr),
            vmem(n_row, n_col - 1, sh2, kr),
            vmem(NSB, n_row, 2, cols, kr),
            vmem(2, 2, tiles_t * th, per_col * TB),
            pltpu.VMEM((n_row, tiles_t * th, kr), F32),
            vmem(n_row, n_col, share_t * th, kr),
            vmem(n_row, n_col - 1, share_t * th, kr),
            dma(7),
            dma(2), dma(2),
            dma(NSB, n_row - 1), dma(NSB, n_row - 1),
            dma(NSB, n_chip), dma(NSB, n_chip),
            dma(NSB, n_chip - 1), dma(NSB, n_chip - 1),
            dma(n_row, n_col - 1), dma(n_row, n_col - 1),
            dma(NSB, n_row - 1), dma(NSB, n_row - 1),
            dma(NSB, n_row), dma(NSB, n_row),
            dma(n_row, n_col - 1), dma(n_row, n_col - 1),
        ],
        compiler_params=pltpu.CompilerParams(
            collective_id=0, has_side_effects=True, vmem_limit_bytes=60 * 1024 * 1024
        ),
    )(
        rhs_super.reshape(NSB, sq_count, TB, width_k),
        factor_super.reshape(NSB, sq_count, TB * per_col, TB),
        mask_super.reshape(NSB, sq_count, per_col),
        dinv_rows.reshape(per_col, TB, -1),
        factor_trail.reshape(tiles_t, TB * per_col, TB),
        mask_trail.reshape(tiles_t, per_col).T,
        rhs_trail.reshape(share_t, 2, th, width_k),
    )
    return solved[:, None], remaining.reshape(rhs_trail.shape)


def body_for(mesh):
    n_row, n_col = mesh.shape["row"], mesh.shape["col"]

    def body(rhs_super, factor_super, mask_super, dinv_rows, factor_trail, mask_trail, rhs_trail):
        args = (rhs_super, factor_super, mask_super, dinv_rows, factor_trail, mask_trail, rhs_trail)
        due_rows = rhs_super.shape[1] * TB
        fits = (
            ST % n_col == 0
            and due_rows % n_col == 0
            and TB % (due_rows // n_col) == 0
            and (due_rows // n_col) % 32 == 0
            and n_col % 2 == 0
            and rhs_super.shape[-1] % (n_row * 128) == 0
        )
        return fast_body(n_row, n_col, *args) if fits else plain_body(*args)

    return body


def solution(mesh):
    placed = (
        P(None, None, "row", None, None),
        P(None, None, "row", None, None, "col", None),
        P(None, None, "row", None, "col"),
        P(None, "col", None, None),
        P(None, "row", None, None, "col", None),
        P(None, "row", None, "col"),
        P("col", None, "row", None, None),
    )
    return jax.shard_map(
        body_for(mesh),
        mesh=mesh,
        in_specs=placed,
        out_specs=(P(None, "col", None, None), P("col", None, "row", None, None)),
        check_vma=False,
    )
```

time: 77 us -> 55 us (0.71)
  Pallas kernels: 67 us -> 50.7 us
  local copies, waits for them, and re-layouts: 9.06 us -> 3.44 us
    pallas_call x1, Pallas kernels: 67 us -> 50.7 us  [fast_body(): pl.pallas_call(functools.partial(kernel, n_row, n_col), out_shape=(jax.Sh...]
    unnamed x14 -> x2, local copies, waits for them, and re-layouts: 8.3 us -> 3.44 us
where the time goes in v2:
time: 55 us; the launch traced here: 54.8 us
  Pallas kernels  50.7 us (92%)
  local copies, waits for them, and re-layouts  3.44 us (6%)
  between operations  0.64 us (1%)
    pallas_call x1, Pallas kernels, fast_body(): pl.pallas_call(functools.partial(kernel, n_row, n_col), out_shape=(jax.Sh...  50.7 us
    unnamed x2, local copies, waits for them, and re-layouts  3.44 us

profile of v2, /device:TPU:0, one launch (start us, length us, event | category | flops | bytes accessed | tf_op | source)
XLA Modules:
  0.0 54.8 jit_solution(12813884075712242152)
XLA Ops:
  0.6 50.7 %shard_map.86 = (bf16[4,128,512]{2,1,0:T(8,128)(2,1)}, bf16[1,2,64,512]{3,2,1,0:T(8,128)(2,1)}) custom-call(bf16[2,4,128,512]{3,2,1,0:T(8,128)(2,1)} %bitcast.14, bf16[2,4,512,128]{3,2,1,0:T(8,128)(2,1)} %bitcast.15, s32[2,4,4]{2,1,0:T(4,128)} %bitcast.20, bf16[4,128,2048]{2,1,0:T(8,128)(2,1)} %bitcast.13, bf16[8,512,128]{2,1,0:T(8,128)(2,1)} %bitcast.16, ...), custom_call_target="tpu_custom_call" | custom-call | tf_op jit(solution)/shard_map/pallas_call | solution.py:303
  51.4 1.9 %copy.12 = bf16[4,1,128,512]{3,2,1,0:T(8,128)(2,1)} copy(bf16[4,1,128,512]{3,2,1,0:T(8,128)(2,1)} %bitcast.17) | data formatting | bytes 1048576
  53.2 1.6 %copy.13 = bf16[1,1,1,128,512]{4,3,2,1,0:T(8,128)(2,1)} copy(bf16[1,1,1,128,512]{4,3,2,1,0:T(8,128)(2,1)} %bitcast.19) | data formatting | bytes 262144
